TPU v7x, 32 devices: a whole 2x2x4 slice. The times are simulated.
32 devices in a mesh: ctx: 4 (over y, x), head: 8 (over z, core).
Axes of the slice: x: 2, y: 2, z: 4, core: 2. Of those that a mesh axis runs over, the one named last changes fastest.
Arguments:
- doc_lengths: int32 [4], replicated, may hold values from 1 to 1536, 2048 in all
- lin_q: bfloat16 [2048, 8192], P('ctx', 'head'), may hold values from -6 to 6
- lin_k: bfloat16 [2048, 8192], P('ctx', 'head'), may hold values from -6 to 6
- lin_v: bfloat16 [2048, 8192], P('ctx', 'head'), may hold values from -40 to 40
- log_decay: float32 [64, 2048], P('head', 'ctx'), may hold values from -1 to 0
- lin_gain: float32 [8192], P('head'), may hold values from 0.5 to 1.5
- soft_q: bfloat16 [2048, 8192], P('ctx', 'head'), may hold values from -48 to 48
- soft_k: bfloat16 [2048, 1024], P('ctx', 'head'), may hold values from -6 to 6
- soft_v: bfloat16 [2048, 1024], P('ctx', 'head'), may hold values from -6 to 6
Outputs:
- lin_out: bfloat16 [2048, 8192], P('ctx', 'head')
- soft_out: bfloat16 [2048, 8192], P('ctx', 'head')
Inputs may be any that keep to these rules, and one draw needn't show every extreme that they name: `doc_lengths`: the 4 lengths sum to 2048 and the largest is exactly 1536.
All inputs are finite; a program needn't handle non-finite values.
Results may differ from a plain program's by a relative error of at most 0.015.
Values may be sent and summed in bfloat16 or wider, within the bound.
No kernel may reach another device: no remote copies, remote signals or barrier semaphores. Data moves between devices by JAX's collectives and lax.ppermute only.
A program may use at most 64 MiB of HBM per device.

v0:
```python
import jax
import jax.numpy as jnp
from jax import lax
from jax.sharding import PartitionSpec as P

KVH = 8
DH = 128
BLK = 256


def prefix(value, axis, join, neutral):
    place = lax.axis_index(axis)
    gathered = jax.tree.map(
        lambda a, kind: lax.all_gather(a.astype(kind), axis), value, (jnp.bfloat16, jnp.bfloat16)
    )
    state = jax.tree.map(lambda a, e: jnp.zeros_like(a) + jnp.asarray(e, a.dtype), value, neutral)

    def one(turn, state):
        return join(
            state,
            jax.tree.map(
                lambda a, own: lax.dynamic_index_in_dim(a, turn, 0, False).astype(own.dtype),
                gathered,
                value,
            ),
        )

    return lax.fori_loop(0, place, one, state)


def swapped(value, axis, stride):
    return lax.ppermute(value, axis, [(i, i ^ 1 << stride) for i in range(lax.axis_size(axis))])


def doc_index(doc_lengths, positions):
    bounds = jnp.cumsum(doc_lengths)
    counted = jnp.sum((bounds[None, :] <= positions[:, None]).astype(jnp.int32), axis=1)
    return jnp.where(positions < 0, -1, counted)


def lightning_parts(queries, keys_block, values_block, decay_block, segs_block, seg_before):
    running = jnp.cumsum(decay_block, axis=1)
    block_len = segs_block.shape[0]
    rows_iota = lax.broadcasted_iota(jnp.int32, (block_len, block_len), 0)
    cols_iota = lax.broadcasted_iota(jnp.int32, (block_len, block_len), 1)
    allowed = (rows_iota >= cols_iota) & (segs_block[:, None] == segs_block[None, :])
    spread = jnp.where(allowed[None], running[:, :, None] - running[:, None, :], 0.0)
    decays = jnp.where(allowed[None], jnp.exp(spread), 0.0)
    scores = (
        jnp.einsum("ihd,jhd->hij", queries, keys_block, preferred_element_type=jnp.float32) * decays
    )
    scores = scores.astype(jnp.bfloat16)
    inside = jnp.einsum("hij,jhd->ihd", scores, values_block, preferred_element_type=jnp.float32)
    carried = (segs_block == seg_before).astype(jnp.float32)
    entering = jnp.exp(running) * carried[None, :]
    closing = running[:, -1:]
    tail_mask = (segs_block == segs_block[-1]).astype(jnp.float32)
    weights = jnp.exp(closing - running) * tail_mask[None, :]
    weighted = (keys_block * weights.T[:, :, None]).astype(jnp.bfloat16)
    update = jnp.einsum("jhd,jhe->hde", weighted, values_block, preferred_element_type=jnp.float32)
    kept_flag = (segs_block[-1] == seg_before).astype(jnp.float32)
    decay_factor = kept_flag * jnp.exp(closing[:, 0])
    return (inside, entering, update, decay_factor)


def local(doc_lengths, lin_q, lin_k, lin_v, log_decay, lin_gain, soft_q, soft_k, soft_v):
    tok_count = lin_q.shape[0]
    heads_here = lin_gain.shape[0] // DH
    ctx_place = lax.axis_index("ctx")
    positions = ctx_place * tok_count + jnp.arange(tok_count, dtype=jnp.int32)
    doc_ids = doc_index(doc_lengths, positions)
    seg_previous = doc_index(doc_lengths, positions[:1] - 1)[0]
    query_rows = lin_q.reshape(tok_count, heads_here, DH)
    key_rows = lin_k.reshape(tok_count, heads_here, DH)
    value_rows = lin_v.reshape(tok_count, heads_here, DH)
    blocks = tok_count // BLK
    pieces_list = []
    local_state = jnp.zeros((heads_here, DH, DH), jnp.float32)
    through = jnp.ones((heads_here,), jnp.float32)
    for number in range(blocks):
        first_row = number * BLK
        last_row = first_row + BLK
        seg_before = seg_previous if number == 0 else doc_ids[first_row - 1]
        parts_now = lightning_parts(
            query_rows[first_row:last_row],
            key_rows[first_row:last_row],
            value_rows[first_row:last_row],
            log_decay[:, first_row:last_row],
            doc_ids[first_row:last_row],
            seg_before,
        )
        pieces_list.append(parts_now)
        local_state = parts_now[3][:, None, None] * local_state + parts_now[2]
        through = through * parts_now[3]
    empty_state = jnp.zeros((heads_here, DH, DH), jnp.float32)

    def combine(earlier, later):
        return (earlier[0] * later[0], later[0][:, None, None] * earlier[1] + later[1])

    incoming = prefix(
        (through, local_state), "ctx", combine, (jnp.ones((heads_here,), jnp.float32), empty_state)
    )
    carry_state = incoming[1]
    outputs = []
    for number in range(blocks):
        first_row = number * BLK
        inside, entering, update, decay_factor = pieces_list[number]
        across = jnp.einsum(
            "ihd,hde->ihe",
            query_rows[first_row : first_row + BLK],
            carry_state.astype(jnp.bfloat16),
            preferred_element_type=jnp.float32,
        )
        outputs.append(inside + across * entering.T[:, :, None])
        carry_state = decay_factor[:, None, None] * carry_state + update
    raw_out = jnp.concatenate(outputs, axis=0)
    norm_scale = lax.rsqrt(jnp.mean(raw_out * raw_out, axis=2, keepdims=True) + 1e-06)
    lin_out = (
        (raw_out * norm_scale * lin_gain.reshape(1, heads_here, DH))
        .reshape(tok_count, heads_here * DH)
        .astype(jnp.bfloat16)
    )
    head_place = lax.axis_index("head")
    group_width = lax.axis_size("head") // KVH
    bit_count = group_width.bit_length() - 1
    own_keys, own_values = (soft_k, soft_v)
    for bit in range(bit_count):
        far_keys, far_values = swapped((own_keys, own_values), "head", bit)
        upper = head_place // (1 << bit) % 2 == 1
        own_keys = jnp.where(
            upper,
            jnp.concatenate([far_keys, own_keys], axis=1),
            jnp.concatenate([own_keys, far_keys], axis=1),
        )
        own_values = jnp.where(
            upper,
            jnp.concatenate([far_values, own_values], axis=1),
            jnp.concatenate([own_values, far_values], axis=1),
        )
    soft_rows = soft_q.reshape(tok_count, heads_here, DH)

    def attend(softmax_state, key_piece, value_piece, key_start):
        row_top, row_total, accum_rows = softmax_state
        key_pos = key_start + jnp.arange(key_piece.shape[0], dtype=jnp.int32)
        key_doc = doc_index(doc_lengths, key_pos)
        scores = jnp.einsum(
            "ihd,jd->hij", soft_rows, key_piece, preferred_element_type=jnp.float32
        ) * DH ** (-0.5)
        allowed = (key_pos[None, :] <= positions[:, None]) & (key_doc[None, :] == doc_ids[:, None])
        masked = jnp.where(allowed[None], scores, -1e30)
        new_top = jnp.maximum(row_top, jnp.max(masked, axis=2))
        exp_terms = jnp.where(allowed[None], jnp.exp(scores - new_top[:, :, None]), 0.0)
        rescale = jnp.exp(row_top - new_top)
        new_total = rescale * row_total + jnp.sum(exp_terms, axis=2)
        new_accum = rescale[:, :, None] * accum_rows + jnp.einsum(
            "hij,jd->hid",
            exp_terms.astype(jnp.bfloat16),
            value_piece,
            preferred_element_type=jnp.float32,
        )
        return (new_top, new_total, new_accum)

    def visit(softmax_state, key_piece, value_piece, key_start):
        return attend(softmax_state, key_piece, value_piece, key_start)

    start_state = (
        jnp.full((heads_here, tok_count), -1e30, jnp.float32),
        jnp.zeros((heads_here, tok_count), jnp.float32),
        jnp.zeros((heads_here, tok_count, DH), jnp.float32),
    )
    key_piece = lax.all_gather(own_keys, "ctx", axis=0, tiled=True)
    value_piece = lax.all_gather(own_values, "ctx", axis=0, tiled=True)
    row_count = key_piece.shape[0]

    def inner_visit(state_in, scan_items):
        offset, key_part, value_part = scan_items
        return (visit(state_in, key_part, value_part, offset), None)

    offsets = jnp.arange(row_count // 512, dtype=jnp.int32) * 512
    result, _ = lax.scan(
        inner_visit,
        start_state,
        (
            offsets,
            key_piece.reshape(row_count // 512, 512, DH),
            value_piece.reshape(row_count // 512, 512, DH),
        ),
    )
    final_top, final_total, final_accum = result
    soft_out = (
        (final_accum / final_total[:, :, None])
        .transpose(1, 0, 2)
        .reshape(tok_count, heads_here * DH)
        .astype(jnp.bfloat16)
    )
    return (lin_out, soft_out)


def solution(mesh):
    placed = (
        P(),
        P("ctx", "head"),
        P("ctx", "head"),
        P("ctx", "head"),
        P("head", "ctx"),
        P("head"),
        P("ctx", "head"),
        P("ctx", "head"),
        P("ctx", "head"),
    )
    return jax.shard_map(
        local,
        mesh=mesh,
        in_specs=placed,
        out_specs=(P("ctx", "head"), P("ctx", "head")),
        check_vma=False,
    )
```

profile of v0, /device:TPU:0, one launch (start us, length us, event | category | flops | bytes accessed | tf_op | source)
XLA Modules:
  0.0 158.2 jit_solution(122099043904819870)
XLA Ops:
  7.7 0.8 reduce-window.19
  9.8 0.7 fusion.52
  11.9 1.3 compare_convert_fusion.2
  14.5 0.7 slice_bitcast_fusion.1
  17.0 1.3 fusion.56
  18.5 1.5 fusion.57
  21.3 1.0 fusion.34
  22.6 0.6 dynamic-slice
  24.1 11.3 %all-reduce = bf16[32]{0:T(256)(128)(2,1)S(1)} all-reduce(bf16[32]{0:T(256)(128)(2,1)S(1)} %dynamic-update-slice), channel_id=2, replica_groups=mesh['ctx'=4,'head'=8] {'ctx'}, use_global_device_ids=true, to_apply=%add | all-reduce | flops 32 | bytes 128
  35.5 1.5 copy.133
  37.1 0.7 copy.134
  37.7 13.1 %all_gather.19 = bf16[2048,128]{1,0:T(8,128)(2,1)S(1)} all-gather(bf16[512,128]{1,0:T(8,128)(2,1)S(1)} %copy-done.15), channel_id=1, replica_groups=mesh['ctx'=4,'head'=8] {'ctx'}, dimensions={0}, use_global_device_ids=true | all-gather | bytes 655360 | tf_op jit(solution)/shard_map/all_gather | solution.py:171
  50.9 10.0 %all_gather.20 = bf16[2048,128]{1,0:T(8,128)(2,1)} all-gather(bf16[512,128]{1,0:T(8,128)(2,1)S(1)} %copy-done.16), channel_id=1, replica_groups=mesh['ctx'=4,'head'=8] {'ctx'}, dimensions={0}, use_global_device_ids=true | all-gather | bytes 655360 | tf_op jit(solution)/shard_map/all_gather | solution.py:172
  61.1 70.8 %while.30 = (s32[]{:T(128)}, f32[8,512]{1,0:T(8,128)S(1)}, f32[8,512]{1,0:T(8,128)S(1)}, f32[8,512,128]{2,1,0:T(8,128)}, s32[4]{0:T(128)S(1)}, /*index=5*/s32[1,...) while((s32[]{:T(128)}, f32[8,512]{1,0:T(8,128)S(1)}, ...), condition=%wide.region_15.16_spmd.clone, body=%wide.region_11.15_spmd.clone.sunk | while | flops 1099198464 | bytes 65557200 | solution.py:180
  61.1 0.7 dynamic_slice.51
  61.7 0.7 iota_add_fusion.4
  62.5 0.7 compare_select_fusion.3
  63.5 4.7 %fusion.82 = (f32[8,512]{1,0:T(8,128)S(1)}, f32[512,512,8]{1,0,2:T(8,128)}) fusion(pred[512,512]{0,1:T(8,128)(4,1)S(1)} %compare_and_fusion.2, bf16[512,8,128]{2,0,1:T(8,128)(2,1)S(1)} %get-tuple-element.504, bf16[4,512,128]{2,1,0:T(8,128)(2,1)S(1)} %get-tuple-element.503, s32[]{:T(128)} %get-tuple-element.483), kind=kOutput, calls=%fused_computation.5.clone.1 | convolution fusion | flops 543158272 | bytes 9846788 | tf_op jit(solution)/shard_map/while/body/eval_jaxpr/ihd,jd->hij/dot_general | solution.py:146
  68.2 5.3 %fusion.83 = f32[8,512]{1,0:T(8,128)S(1)} fusion(f32[512,512,8]{1,0,2:T(8,128)} %get-tuple-element.443, f32[8,512]{1,0:T(8,128)S(1)} %select_maximum_fusion.2, pred[512,512]{0,1:T(8,128)(4,1)S(1)} %compare_and_fusion.2), kind=kLoop, calls=%fused_computation.9.clone.1 | loop fusion | flops 8384512 | bytes 8683520 | tf_op jit(solution)/shard_map/while/body/eval_jaxpr/reduce_sum | solution.py:154
  74.0 4.5 %fusion.85 = f32[8,512,128]{2,1,0:T(8,128)} fusion(f32[8,512,128]{2,1,0:T(8,128)} %get-tuple-element.486, f32[512,512,8]{1,0,2:T(8,128)S(1)} %copy-done, f32[8,512]{1,0:T(8,128)S(1)} %select_maximum_fusion.2, pred[512,512]{0,1:T(8,128)(4,1)S(1)} %compare_and_fusion.2, f32[8,512]{1,0:T(8,128)S(1)} %get-tuple-element.445, pred[]{:T(512)S(6)} %compare.3, ...), kind=kOutput, calls=%fused_computation.13.clone.1 | convolution fusion | flops 546832384 | bytes 13009409 | tf_op jit(solution)/shard_map/while/body/eval_jaxpr/hij,jd->hid/dot_general | solution.py:155
  78.5 0.7 dynamic_slice.51
  79.2 0.7 iota_add_fusion.4
  80.0 0.7 compare_select_fusion.3
  81.0 4.7 %fusion.82 = (f32[8,512]{1,0:T(8,128)S(1)}, f32[512,512,8]{1,0,2:T(8,128)}) fusion(pred[512,512]{0,1:T(8,128)(4,1)S(1)} %compare_and_fusion.2, bf16[512,8,128]{2,0,1:T(8,128)(2,1)S(1)} %get-tuple-element.504, bf16[4,512,128]{2,1,0:T(8,128)(2,1)S(1)} %get-tuple-element.503, s32[]{:T(128)} %get-tuple-element.483), kind=kOutput, calls=%fused_computation.5.clone.1 | convolution fusion | flops 543158272 | bytes 9846788 | tf_op jit(solution)/shard_map/while/body/eval_jaxpr/ihd,jd->hij/dot_general | solution.py:146
  85.7 5.3 %fusion.83 = f32[8,512]{1,0:T(8,128)S(1)} fusion(f32[512,512,8]{1,0,2:T(8,128)} %get-tuple-element.443, f32[8,512]{1,0:T(8,128)S(1)} %select_maximum_fusion.2, pred[512,512]{0,1:T(8,128)(4,1)S(1)} %compare_and_fusion.2), kind=kLoop, calls=%fused_computation.9.clone.1 | loop fusion | flops 8384512 | bytes 8683520 | tf_op jit(solution)/shard_map/while/body/eval_jaxpr/reduce_sum | solution.py:154
  91.4 4.9 %fusion.85 = f32[8,512,128]{2,1,0:T(8,128)} fusion(f32[8,512,128]{2,1,0:T(8,128)} %get-tuple-element.486, f32[512,512,8]{1,0,2:T(8,128)S(1)} %copy-done, f32[8,512]{1,0:T(8,128)S(1)} %select_maximum_fusion.2, pred[512,512]{0,1:T(8,128)(4,1)S(1)} %compare_and_fusion.2, f32[8,512]{1,0:T(8,128)S(1)} %get-tuple-element.445, pred[]{:T(512)S(6)} %compare.3, ...), kind=kOutput, calls=%fused_computation.13.clone.1 | convolution fusion | flops 546832384 | bytes 13009409 | tf_op jit(solution)/shard_map/while/body/eval_jaxpr/hij,jd->hid/dot_general | solution.py:155
  96.3 0.7 dynamic_slice.51
  97.0 0.7 iota_add_fusion.4
  97.7 0.7 compare_select_fusion.3
  98.7 4.7 %fusion.82 = (f32[8,512]{1,0:T(8,128)S(1)}, f32[512,512,8]{1,0,2:T(8,128)}) fusion(pred[512,512]{0,1:T(8,128)(4,1)S(1)} %compare_and_fusion.2, bf16[512,8,128]{2,0,1:T(8,128)(2,1)S(1)} %get-tuple-element.504, bf16[4,512,128]{2,1,0:T(8,128)(2,1)S(1)} %get-tuple-element.503, s32[]{:T(128)} %get-tuple-element.483), kind=kOutput, calls=%fused_computation.5.clone.1 | convolution fusion | flops 543158272 | bytes 9846788 | tf_op jit(solution)/shard_map/while/body/eval_jaxpr/ihd,jd->hij/dot_general | solution.py:146
  103.4 5.3 %fusion.83 = f32[8,512]{1,0:T(8,128)S(1)} fusion(f32[512,512,8]{1,0,2:T(8,128)} %get-tuple-element.443, f32[8,512]{1,0:T(8,128)S(1)} %select_maximum_fusion.2, pred[512,512]{0,1:T(8,128)(4,1)S(1)} %compare_and_fusion.2), kind=kLoop, calls=%fused_computation.9.clone.1 | loop fusion | flops 8384512 | bytes 8683520 | tf_op jit(solution)/shard_map/while/body/eval_jaxpr/reduce_sum | solution.py:154
  109.2 4.9 %fusion.85 = f32[8,512,128]{2,1,0:T(8,128)} fusion(f32[8,512,128]{2,1,0:T(8,128)} %get-tuple-element.486, f32[512,512,8]{1,0,2:T(8,128)S(1)} %copy-done, f32[8,512]{1,0:T(8,128)S(1)} %select_maximum_fusion.2, pred[512,512]{0,1:T(8,128)(4,1)S(1)} %compare_and_fusion.2, f32[8,512]{1,0:T(8,128)S(1)} %get-tuple-element.445, pred[]{:T(512)S(6)} %compare.3, ...), kind=kOutput, calls=%fused_computation.13.clone.1 | convolution fusion | flops 546832384 | bytes 13009409 | tf_op jit(solution)/shard_map/while/body/eval_jaxpr/hij,jd->hid/dot_general | solution.py:155
  114.1 0.7 dynamic_slice.51
  114.7 0.7 iota_add_fusion.4
  115.5 0.7 compare_select_fusion.3
  116.5 4.7 %fusion.82 = (f32[8,512]{1,0:T(8,128)S(1)}, f32[512,512,8]{1,0,2:T(8,128)}) fusion(pred[512,512]{0,1:T(8,128)(4,1)S(1)} %compare_and_fusion.2, bf16[512,8,128]{2,0,1:T(8,128)(2,1)S(1)} %get-tuple-element.504, bf16[4,512,128]{2,1,0:T(8,128)(2,1)S(1)} %get-tuple-element.503, s32[]{:T(128)} %get-tuple-element.483), kind=kOutput, calls=%fused_computation.5.clone.1 | convolution fusion | flops 543158272 | bytes 9846788 | tf_op jit(solution)/shard_map/while/body/eval_jaxpr/ihd,jd->hij/dot_general | solution.py:146
  121.2 5.3 %fusion.83 = f32[8,512]{1,0:T(8,128)S(1)} fusion(f32[512,512,8]{1,0,2:T(8,128)} %get-tuple-element.443, f32[8,512]{1,0:T(8,128)S(1)} %select_maximum_fusion.2, pred[512,512]{0,1:T(8,128)(4,1)S(1)} %compare_and_fusion.2), kind=kLoop, calls=%fused_computation.9.clone.1 | loop fusion | flops 8384512 | bytes 8683520 | tf_op jit(solution)/shard_map/while/body/eval_jaxpr/reduce_sum | solution.py:154
  127.0 4.9 %fusion.85 = f32[8,512,128]{2,1,0:T(8,128)} fusion(f32[8,512,128]{2,1,0:T(8,128)} %get-tuple-element.486, f32[512,512,8]{1,0,2:T(8,128)S(1)} %copy-done, f32[8,512]{1,0:T(8,128)S(1)} %select_maximum_fusion.2, pred[512,512]{0,1:T(8,128)(4,1)S(1)} %compare_and_fusion.2, f32[8,512]{1,0:T(8,128)S(1)} %get-tuple-element.445, pred[]{:T(512)S(6)} %compare.3, ...), kind=kOutput, calls=%fused_computation.13.clone.1 | convolution fusion | flops 546832384 | bytes 13009409 | tf_op jit(solution)/shard_map/while/body/eval_jaxpr/hij,jd->hid/dot_general | solution.py:155
  131.8 1.4 fusion.55
  133.2 1.0 copy.147
  134.6 3.1 %fusion.27 = f32[256,8,128]{0,2,1:T(8,128)} fusion(bf16[256,8,128]{0,2,1:T(8,128)(2,1)S(1)} %bitcast.141, bf16[256,8,128]{0,2,1:T(8,128)(2,1)} %bitcast.148, bf16[256,8,128]{0,2,1:T(8,128)(2,1)S(1)} %bitcast.139, f32[8,256]{1,0:T(8,128)S(1)} %get-tuple-element.332, pred[256,256]{1,0:T(8,128)(4,1)S(1)} %get-tuple-element.334), kind=kOutput, calls=%fused_computation.41 | convolution fusion | flops 271056896 | bytes 2695168 | tf_op jit(solution)/shard_map/hij,jhd->ihd/dot_general | solution.py:53
  137.7 1.9 %fusion.29 = f32[256,8,128]{0,2,1:T(8,128)} fusion(bf16[256,8,128]{0,2,1:T(8,128)(2,1)S(1)} %bitcast.145, bf16[256,8,128]{0,2,1:T(8,128)(2,1)S(1)} %bitcast.146, bf16[256,8,128]{0,2,1:T(8,128)(2,1)S(1)} %bitcast.143, f32[8,256]{1,0:T(8,128)S(1)} %get-tuple-element.310, pred[256,256]{1,0:T(8,128)(4,1)S(1)} %get-tuple-element.333), kind=kOutput, calls=%fused_computation.43 | convolution fusion | flops 271056896 | bytes 2695168 | tf_op jit(solution)/shard_map/hij,jhd->ihd/dot_general | solution.py:53
  139.7 2.7 %copy_bitcast_fusion = bf16[512,1024]{1,0:T(8,128)(2,1)} fusion(f32[8,512,128]{2,1,0:T(8,128)} %get-tuple-element.175, f32[8,512]{1,0:T(8,128)S(1)} %get-tuple-element.176), kind=kLoop, calls=%fused_computation.52 | loop fusion | flops 1048576 | bytes 3162112 | tf_op jit(solution)/shard_map/convert_element_type | solution.py:194
  142.7 0.8 copy-done.13
  143.5 1.6 fusion.33
  145.8 1.3 copy.130
  147.2 1.3 copy.131
  149.7 1.7 %fusion.24 = bf16[512,1024]{1,0:T(8,128)(2,1)} fusion(f32[64,8,8,128]{3,2,1,0:T(8,128)S(1)} %bitcast.135, f32[256,1024]{1,0:T(8,128)S(1)} %copy-done.2, f32[256,1024]{1,0:T(8,128)S(1)} %copy-done.1, f32[1024]{0:T(1024)S(1)} %copy-done.17), kind=kLoop, calls=%fused_computation.34 | loop fusion | flops 2097152 | bytes 5246976 | tf_op jit(solution)/shard_map/convert_element_type | solution.py:121
  (112 shorter events, 11.3 us)
Async XLA Ops:
  7.2 135.2 %all-gather.4.cloned.1.call-start = ((), (), s32[]{:S(2)}) async-start(), calls=%async_computation | async-start | bytes 1310720 | tf_op jit(solution)/shard_map/all_gather | solution.py:14
  18.5 2.5 %copy-start.3 = (bf16[256,1024]{0,1:T(8,128)(2,1)}, bf16[256,1024]{0,1:T(8,128)(2,1)S(1)}, u32[]{:S(2)}) copy-start(bf16[256,1024]{0,1:T(8,128)(2,1)S(1)} %copy.148) | copy-start | bytes 1572868
  20.2 2.2 %copy-start.5 = (bf16[256,1024]{0,1:T(8,128)(2,1)}, bf16[256,1024]{0,1:T(8,128)(2,1)S(1)}, u32[]{:S(2)}) copy-start(bf16[256,1024]{0,1:T(8,128)(2,1)S(1)} %copy.118) | copy-start | bytes 1572868
  20.7 1.6 %copy-start.7 = (bf16[256,1024]{0,1:T(8,128)(2,1)}, bf16[256,1024]{0,1:T(8,128)(2,1)S(1)}, u32[]{:S(2)}) copy-start(bf16[256,1024]{0,1:T(8,128)(2,1)S(1)} %copy.149) | copy-start | bytes 1572868
  21.0 14.5 %copy-start.9 = (bf16[256,1024]{0,1:T(8,128)(2,1)}, bf16[256,1024]{0,1:T(8,128)(2,1)S(1)}, u32[]{:S(2)}) copy-start(bf16[256,1024]{0,1:T(8,128)(2,1)S(1)} %copy.150) | copy-start | bytes 1572868
  21.0 1.6 %copy-start.19 = (u32[32]{0:T(128)S(1)}, u32[32]{0:T(128)}, u32[]{:S(2)}) copy-start(u32[32]{0:T(128)} %constant.96) | copy-start | bytes 388
  35.5 2.2 %copy-start.15 = (bf16[512,128]{1,0:T(8,128)(2,1)S(1)}, bf16[512,128]{1,0:T(8,128)(2,1)}, u32[]{:S(2)}) copy-start(bf16[512,128]{1,0:T(8,128)(2,1)} %param.20) | copy-start | bytes 393220
  35.5 15.4 %copy-start.16 = (bf16[512,128]{1,0:T(8,128)(2,1)S(1)}, bf16[512,128]{1,0:T(8,128)(2,1)}, u32[]{:S(2)}) copy-start(bf16[512,128]{1,0:T(8,128)(2,1)} %param.21) | copy-start | bytes 393220
  37.1 23.8 %copy-start.18 = (s32[4]{0:T(128)S(1)}, s32[4]{0:T(128)}, u32[]{:S(2)}) copy-start(s32[4]{0:T(128)} %param.13) | copy-start | bytes 52
  68.2 5.8 %copy-start = (f32[512,512,8]{1,0,2:T(8,128)S(1)}, f32[512,512,8]{1,0,2:T(8,128)}, u32[]{:S(2)}) copy-start(f32[512,512,8]{1,0,2:T(8,128)} %get-tuple-element.443) | copy-start | bytes 25165828 | tf_op jit(solution)/shard_map/while
  85.7 5.8 %copy-start = (f32[512,512,8]{1,0,2:T(8,128)S(1)}, f32[512,512,8]{1,0,2:T(8,128)}, u32[]{:S(2)}) copy-start(f32[512,512,8]{1,0,2:T(8,128)} %get-tuple-element.443) | copy-start | bytes 25165828 | tf_op jit(solution)/shard_map/while
  103.4 5.8 %copy-start = (f32[512,512,8]{1,0,2:T(8,128)S(1)}, f32[512,512,8]{1,0,2:T(8,128)}, u32[]{:S(2)}) copy-start(f32[512,512,8]{1,0,2:T(8,128)} %get-tuple-element.443) | copy-start | bytes 25165828 | tf_op jit(solution)/shard_map/while
  121.2 5.8 %copy-start = (f32[512,512,8]{1,0,2:T(8,128)S(1)}, f32[512,512,8]{1,0,2:T(8,128)}, u32[]{:S(2)}) copy-start(f32[512,512,8]{1,0,2:T(8,128)} %get-tuple-element.443) | copy-start | bytes 25165828 | tf_op jit(solution)/shard_map/while
  131.8 2.8 %copy-start.4 = (bf16[256,1024]{0,1:T(8,128)(2,1)S(1)}, bf16[256,1024]{0,1:T(8,128)(2,1)}, u32[]{:S(2)}) copy-start(bf16[256,1024]{0,1:T(8,128)(2,1)} %copy-done.3) | copy-start | bytes 1572868
  131.8 2.8 %copy-start.6 = (bf16[256,1024]{0,1:T(8,128)(2,1)S(1)}, bf16[256,1024]{0,1:T(8,128)(2,1)}, u32[]{:S(2)}) copy-start(bf16[256,1024]{0,1:T(8,128)(2,1)} %copy-done.5) | copy-start | bytes 1572868
  134.4 3.3 %copy-start.11 = (bf16[256,1024]{0,1:T(8,128)(2,1)}, bf16[256,1024]{0,1:T(8,128)(2,1)S(1)}, u32[]{:S(2)}) copy-start(bf16[256,1024]{0,1:T(8,128)(2,1)S(1)} %copy.151) | copy-start | bytes 1572868
  134.6 3.1 %copy-start.8 = (bf16[256,1024]{0,1:T(8,128)(2,1)S(1)}, bf16[256,1024]{0,1:T(8,128)(2,1)}, u32[]{:S(2)}) copy-start(bf16[256,1024]{0,1:T(8,128)(2,1)} %copy-done.7) | copy-start | bytes 1572868
  134.6 3.1 %copy-start.10 = (bf16[256,1024]{0,1:T(8,128)(2,1)S(1)}, bf16[256,1024]{0,1:T(8,128)(2,1)}, u32[]{:S(2)}) copy-start(bf16[256,1024]{0,1:T(8,128)(2,1)} %copy-done.9) | copy-start | bytes 1572868
  142.4 1.0 copy-start.13
  142.6 2.4 %copy-start.12 = (bf16[256,1024]{0,1:T(8,128)(2,1)S(1)}, bf16[256,1024]{0,1:T(8,128)(2,1)}, u32[]{:S(2)}) copy-start(bf16[256,1024]{0,1:T(8,128)(2,1)} %copy-done.11) | copy-start | bytes 1572868
  142.6 2.4 %copy-start.14 = (f32[256,8,128]{0,2,1:T(8,128)S(1)}, f32[256,8,128]{0,2,1:T(8,128)}, u32[]{:S(2)}) copy-start(f32[256,8,128]{0,2,1:T(8,128)} %fusion.29) | copy-start | bytes 3145732
  147.2 1.9 %copy-start.1 = (f32[256,1024]{1,0:T(8,128)S(1)}, f32[256,1024]{1,0:T(8,128)}, u32[]{:S(2)}) copy-start(f32[256,1024]{1,0:T(8,128)} %copy.130) | copy-start | bytes 3145732
  147.2 1.9 %copy-start.17 = (f32[1024]{0:T(1024)S(1)}, f32[1024]{0:T(1024)}, u32[]{:S(2)}) copy-start(f32[1024]{0:T(1024)} %param.18) | copy-start | bytes 12292
  148.5 1.2 copy-start.2
Sparse Core Ops, SparseCore 0:
  22.5 31.7 all-gather.3
where the time goes:
time: 160 us; the launch traced here: 158 us
  matrix products  46.3 us (29%)
  other arithmetic  37.5 us (23%)
  blocking collectives  34.5 us (22%)
  local copies, waits for them, and re-layouts  21.3 us (13%)
  between operations  18.2 us (11%)
    reduce_sum x4, other arithmetic, attend(): new_total = rescale * row_total + jnp.sum(exp_terms, axis=2)  21 us
    dot_general x4, matrix products, attend(): jnp.einsum('hij,jd->hid', exp_terms.astype(jnp.bfloat16), value_piece, pr...  19.1 us
    dot_general x4, matrix products, attend(): jnp.einsum('ihd,jd->hij', soft_rows, key_piece, preferred_element_type=jn...  18.8 us
    all_gather x1, blocking collectives, local(): key_piece = lax.all_gather(own_keys, 'ctx', axis=0, tiled=True)  13.1 us
    unnamed x1, blocking collectives  11.3 us
    all_gather x1, blocking collectives, local(): value_piece = lax.all_gather(own_values, 'ctx', axis=0, tiled=True)  10 us
    unnamed x48, local copies, waits for them, and re-layouts  6.4 us
    dot_general x2, matrix products, lightning_parts(): jnp.einsum('hij,jhd->ihd', scores, values_block, preferred_element_type=j...  5 us
  transfers between devices with their start and end apart: 1, of which 0 were waited for; matrix products, arithmetic and copies ran while one was open for 52% of the time, Pallas kernels for 0%

commit v1 on v0

v1 whole, which is shorter than its diff:
```python
import functools

import jax
import jax.numpy as jnp
from jax import lax
from jax.experimental import pallas as pl
from jax.experimental.pallas import tpu as pltpu
from jax.sharding import PartitionSpec as P

KVH = 8
DH = 128
BLK = 256
KEYS = 512
LOW = -1e30
LOG2E = 1.4426950408889634
F32 = jnp.float32
BF16 = jnp.bfloat16
NT = (((1,), (1,)), ((), ()))
TN = (((0,), (0,)), ((), ()))
SMEM = pl.BlockSpec(memory_space=pltpu.SMEM)
ANY = pl.BlockSpec(memory_space=pl.ANY)


def swapped(value, axis, bit):
    return lax.ppermute(value, axis, [(i, i ^ 1 << bit) for i in range(lax.axis_size(axis))])


def bounds_of(lengths_ref):
    out, total = [], 0
    for d in range(lengths_ref.shape[0]):
        total = total + lengths_ref[d]
        out.append(total)
    return out


def doc_start(bounds, position):
    start = jnp.zeros_like(position)
    for bound in bounds:
        start = jnp.where(bound <= position, bound, start)
    return start


def log_sums(decay):
    rows = lax.broadcasted_iota(jnp.int32, (BLK, BLK), 0)
    cols = lax.broadcasted_iota(jnp.int32, (BLK, BLK), 1)
    upper = (rows <= cols).astype(F32)
    return jnp.dot(decay, upper, precision=lax.Precision.HIGHEST, preferred_element_type=F32)


def column(row_form, head):
    return jnp.transpose(row_form, (1, 0))[:, head : head + 1]


def states_kernel(lengths_ref, keys_ref, values_ref, decay_ref, msg_ref, first_ref):
    heads = decay_ref.shape[0]
    tokens = keys_ref.shape[0]
    base = lax.axis_index("ctx") * tokens
    bounds = bounds_of(lengths_ref)
    place = lax.broadcasted_iota(jnp.int32, (BLK, 1), 0)
    state = [None] * heads
    through = jnp.ones((heads, 1), F32)
    for b in range(tokens // BLK):
        s = base + b * BLK
        start_last = doc_start(bounds, s + BLK - 1)
        kept = jnp.where(start_last < s, 1.0, 0.0).astype(F32)
        sums = log_sums(decay_ref[:, b * BLK : (b + 1) * BLK])
        closing = sums[:, BLK - 1 : BLK]
        weights = jnp.transpose(jnp.exp(closing - sums), (1, 0))
        weights = jnp.where(s + place >= start_last, weights, 0.0)
        factor = kept * jnp.exp(closing)
        through = through * factor
        for h in range(heads):
            cols = slice(h * DH, (h + 1) * DH)
            keys = keys_ref[b * BLK : (b + 1) * BLK, cols].astype(F32)
            weighted = (keys * weights[:, h : h + 1]).astype(BF16)
            update = lax.dot_general(
                weighted, values_ref[b * BLK : (b + 1) * BLK, cols], TN, preferred_element_type=F32
            )
            if b == 0:
                state[h] = update
            else:
                state[h] = factor[h : h + 1, :] * state[h] + update
            if b < tokens // BLK - 1:
                first_ref[b, h * DH : (h + 1) * DH, :] = update.astype(BF16)
    for h in range(heads):
        msg_ref[h * DH : (h + 1) * DH, :] = state[h].astype(BF16)
    high = through.astype(BF16)
    low = (through - high.astype(F32)).astype(BF16)
    tail = jnp.concatenate([high.astype(F32), low.astype(F32)], axis=0)
    tail = jnp.broadcast_to(tail, (2 * heads, DH))
    extra = msg_ref.shape[0] - heads * DH
    if extra > 2 * heads:
        tail = jnp.concatenate([tail, jnp.zeros((extra - 2 * heads, DH), F32)], axis=0)
    msg_ref[heads * DH :, :] = tail.astype(BF16)


def inside_kernel(lengths_ref, queries_ref, keys_ref, values_ref, decay_ref, out_ref):
    heads = decay_ref.shape[0]
    tokens = keys_ref.shape[0]
    base = lax.axis_index("ctx") * tokens
    bounds = bounds_of(lengths_ref)
    rows = lax.broadcasted_iota(jnp.int32, (BLK, BLK), 0)
    cols = lax.broadcasted_iota(jnp.int32, (BLK, BLK), 1)
    place = lax.broadcasted_iota(jnp.int32, (BLK, 1), 0)
    for b in range(tokens // BLK):
        s = base + b * BLK
        start = doc_start(bounds, s + place) - s
        allowed = (cols <= rows) & (cols >= start)
        sums = log_sums(decay_ref[:, b * BLK : (b + 1) * BLK])
        down = jnp.transpose(sums, (1, 0))
        here = slice(b * BLK, (b + 1) * BLK)
        for h in range(heads):
            there = slice(h * DH, (h + 1) * DH)
            spread = jnp.where(allowed, down[:, h : h + 1] - sums[h : h + 1, :], LOW)
            scores = lax.dot_general(
                queries_ref[here, there], keys_ref[here, there], NT, preferred_element_type=F32
            )
            scores = (scores * jnp.exp(spread)).astype(BF16)
            out_ref[here, there] = jnp.dot(
                scores, values_ref[here, there], preferred_element_type=F32
            ).astype(BF16)


def through_of(msg_ref, heads, h):
    high = msg_ref[heads * DH + h : heads * DH + h + 1, :].astype(F32)
    low = msg_ref[heads * DH + heads + h : heads * DH + heads + h + 1, :].astype(F32)
    return high + low


def combine_kernel(heads, bit, total_ref, prefix_ref, far_ref, new_total_ref, new_prefix_ref):
    upper = (lax.axis_index("ctx") // (1 << bit)) % 2 == 1

    def joined(early_ref, late_ref, out_ref):
        tails = []
        for h in range(heads):
            here = slice(h * DH, (h + 1) * DH)
            late = through_of(late_ref, heads, h)
            early = through_of(early_ref, heads, h)
            out_ref[here, :] = (
                late * early_ref[here, :].astype(F32) + late_ref[here, :].astype(F32)
            ).astype(BF16)
            tails.append(late * early)
        tail = jnp.concatenate(tails, axis=0)
        high = tail.astype(BF16).astype(F32)
        pieces = [high, tail - high]
        extra = out_ref.shape[0] - heads * DH - 2 * heads
        if extra:
            pieces.append(jnp.zeros((extra, DH), F32))
        out_ref[heads * DH :, :] = jnp.concatenate(pieces, axis=0).astype(BF16)

    @pl.when(upper)
    def _():
        joined(far_ref, total_ref, new_total_ref)
        if prefix_ref is None:
            new_prefix_ref[...] = far_ref[...]
        else:
            joined(far_ref, prefix_ref, new_prefix_ref)

    @pl.when(jnp.logical_not(upper))
    def _():
        joined(total_ref, far_ref, new_total_ref)
        if prefix_ref is None:
            new_prefix_ref[...] = jnp.zeros_like(new_prefix_ref)
            new_prefix_ref[heads * DH : heads * DH + 16, :] = jnp.where(
                lax.broadcasted_iota(jnp.int32, (16, DH), 0) < heads, 1.0, 0.0
            ).astype(BF16)
        else:
            new_prefix_ref[...] = prefix_ref[...]


def across_kernel(bit, lengths_ref, queries_ref, inside_ref, decay_ref, gain_ref, first_ref, prefix_ref, far_ref, out_ref):
    heads = decay_ref.shape[0]
    tokens = queries_ref.shape[0]
    place_ctx = lax.axis_index("ctx")
    base = place_ctx * tokens
    upper = jnp.where((place_ctx // (1 << bit)) % 2 == 1, 1.0, 0.0).astype(F32)
    bounds = bounds_of(lengths_ref)
    place = lax.broadcasted_iota(jnp.int32, (BLK, 1), 0)
    state = []
    for h in range(heads):
        here = slice(h * DH, (h + 1) * DH)
        late = upper * through_of(prefix_ref, heads, h)
        own = prefix_ref[here, :].astype(F32)
        state.append(own + jnp.where(upper > 0, late * far_ref[here, :].astype(F32), 0.0))
    for b in range(tokens // BLK):
        s = base + b * BLK
        here = slice(b * BLK, (b + 1) * BLK)
        start_last = doc_start(bounds, s + BLK - 1)
        kept = jnp.where(start_last < s, 1.0, 0.0).astype(F32)
        sums = log_sums(decay_ref[:, here])
        factor = kept * jnp.exp(sums[:, BLK - 1 : BLK])
        entering = jnp.exp(jnp.transpose(sums, (1, 0)))
        entering = jnp.where(doc_start(bounds, s + place) < s, entering, 0.0)
        for h in range(heads):
            there = slice(h * DH, (h + 1) * DH)
            across = jnp.dot(queries_ref[here, there], state[h].astype(BF16), preferred_element_type=F32)
            raw = inside_ref[here, there].astype(F32) + across * entering[:, h : h + 1]
            scale = lax.rsqrt(jnp.mean(raw * raw, axis=1, keepdims=True) + 1e-06)
            out_ref[here, there] = (raw * scale * gain_ref[:, there]).astype(BF16)
            if b < tokens // BLK - 1:
                state[h] = factor[h : h + 1, :] * state[h] + first_ref[b, there, :].astype(F32)


def softmax_kernel(count, lengths_ref, queries_ref, *refs):
    pieces = refs[:count]
    out_ref, keys, values, scores, tops, totals, sems = refs[count:]
    tokens = queries_ref.shape[0]
    heads = queries_ref.shape[1] // DH
    place_ctx = lax.axis_index("ctx")
    base = place_ctx * tokens
    copies = []
    for m in range(count):
        origin = jnp.int32(0)
        bit = 1
        while bit < count:
            mine = (place_ctx // bit) % 2
            origin = origin + bit * (1 - mine if m & bit else mine)
            bit *= 2
        at = pl.ds(pl.multiple_of(origin * tokens, tokens), tokens)
        copies.append(pltpu.make_async_copy(pieces[m].at[:, :DH], keys.at[at, :], sems.at[0, m]))
        copies.append(pltpu.make_async_copy(pieces[m].at[:, DH:], values.at[at, :DH], sems.at[1, m]))
    for copy in copies:
        copy.start()
    values[:, DH:] = jnp.ones((values.shape[0], DH), BF16)
    for copy in copies:
        copy.wait()
    bounds = bounds_of(lengths_ref)
    place = lax.broadcasted_iota(jnp.int32, (BLK, 1), 0)
    spots = lax.broadcasted_iota(jnp.int32, (BLK, KEYS), 1)
    factor = LOG2E * DH**-0.5

    for block in range(tokens // BLK):
        here = slice(block * BLK, (block + 1) * BLK)
        s = base + block * BLK
        row_start = doc_start(bounds, s + place)
        start_last = doc_start(bounds, s + BLK - 1)
        low = doc_start(bounds, s) // KEYS
        high = (s + BLK + KEYS - 1) // KEYS

        def scored(h, slot):
            query = queries_ref[here, pl.ds(pl.multiple_of(h * DH, DH), DH)]
            tops[...] = jnp.full_like(tops, LOW)

            def step(kb, _):
                first = pl.multiple_of(kb * KEYS, KEYS)
                found = lax.dot_general(query, keys[pl.ds(first, KEYS), :], NT, preferred_element_type=F32)
                whole = (first >= start_last) & (first + KEYS <= s)

                def keep(value):
                    scores[slot, :, pl.ds(first, KEYS)] = value
                    top = tops[...]
                    for part in range(KEYS // 128):
                        top = jnp.maximum(top, value[:, part * 128 : (part + 1) * 128])
                    tops[...] = top

                @pl.when(whole)
                def _():
                    keep(found)

                @pl.when(jnp.logical_not(whole))
                def _():
                    spot = first + spots
                    keep(jnp.where((spot >= row_start) & (spot <= s + place), found, LOW))

                return 0

            lax.fori_loop(low, high, step, 0)
            return jnp.max(tops[...], axis=1, keepdims=True) * factor

        def summed(h, slot, top):
            totals[...] = jnp.zeros_like(totals)

            def step(kb, _):
                first = pl.multiple_of(kb * KEYS, KEYS)
                weights = jnp.exp2(scores[slot, :, pl.ds(first, KEYS)] * factor - top).astype(BF16)
                totals[...] += jnp.dot(weights, values[pl.ds(first, KEYS), :], preferred_element_type=F32)
                return 0

            lax.fori_loop(low, high, step, 0)
            out_ref[here, pl.ds(pl.multiple_of(h * DH, DH), DH)] = (totals[:, :DH] / totals[:, DH:]).astype(BF16)

        def one(h, _):
            top = scored(h, 0)
            summed(h, 0, top)
            return 0

        lax.fori_loop(0, heads, one, 0)


def local(doc_lengths, lin_q, lin_k, lin_v, log_decay, lin_gain, soft_q, soft_k, soft_v):
    tokens = lin_q.shape[0]
    heads = lin_gain.shape[0] // DH
    count = lax.axis_size("ctx")
    bits = count.bit_length() - 1
    blocks = tokens // BLK

    head_place = lax.axis_index("head")
    own_keys, own_values = soft_k, soft_v
    for bit in range((lax.axis_size("head") // KVH).bit_length() - 1):
        far_keys, far_values = swapped((own_keys, own_values), "head", bit)
        upper = head_place // (1 << bit) % 2 == 1

        def beside(own, far):
            return jnp.where(upper, jnp.concatenate([far, own], axis=1), jnp.concatenate([own, far], axis=1))

        own_keys, own_values = beside(own_keys, far_keys), beside(own_values, far_values)
    pieces = [jnp.concatenate([own_keys, own_values], axis=1)]
    for bit in range(bits):
        pieces = pieces + [swapped(piece, "ctx", bit) for piece in pieces]

    msg_rows = heads * DH + -(-2 * heads // 16) * 16
    msg = jax.ShapeDtypeStruct((msg_rows, DH), BF16)
    total, first = pl.pallas_call(
        states_kernel,
        out_shape=(msg, jax.ShapeDtypeStruct((max(blocks - 1, 1), heads * DH, DH), BF16)),
        in_specs=[SMEM] + [pl.BlockSpec(memory_space=pltpu.VMEM)] * 3,
        out_specs=(pl.BlockSpec(memory_space=pltpu.VMEM),) * 2,
        name="states",
    )(doc_lengths, lin_k, lin_v, log_decay)

    inside = pl.pallas_call(
        inside_kernel,
        out_shape=jax.ShapeDtypeStruct(lin_q.shape, BF16),
        in_specs=[SMEM] + [pl.BlockSpec(memory_space=pltpu.VMEM)] * 4,
        out_specs=pl.BlockSpec(memory_space=pltpu.VMEM),
        name="inside",
    )(doc_lengths, lin_q, lin_k, lin_v, log_decay)

    prefix = None
    for bit in range(bits - 1):
        far = swapped(total, "ctx", bit)
        if prefix is None:
            def body(t, f, nt, np_, bit=bit):
                combine_kernel(heads, bit, t, None, f, nt, np_)
            operands = (total, far)
        else:
            body = functools.partial(combine_kernel, heads, bit)
            operands = (total, prefix, far)
        total, prefix = pl.pallas_call(
            body,
            out_shape=(msg, msg),
            in_specs=[pl.BlockSpec(memory_space=pltpu.VMEM)] * len(operands),
            out_specs=(pl.BlockSpec(memory_space=pltpu.VMEM),) * 2,
            name="combine",
        )(*operands)
    far = swapped(total, "ctx", bits - 1)

    soft_out = pl.pallas_call(
        functools.partial(softmax_kernel, count),
        out_shape=jax.ShapeDtypeStruct(soft_q.shape, BF16),
        in_specs=[SMEM, pl.BlockSpec(memory_space=pltpu.VMEM)] + [ANY] * count,
        out_specs=pl.BlockSpec(memory_space=pltpu.VMEM),
        scratch_shapes=[
            pltpu.VMEM((count * tokens, DH), BF16),
            pltpu.VMEM((count * tokens, 2 * DH), BF16),
            pltpu.VMEM((1, BLK, count * tokens), F32),
            pltpu.VMEM((BLK, 128), F32),
            pltpu.VMEM((BLK, 2 * DH), F32),
            pltpu.SemaphoreType.DMA((2, count)),
        ],
        compiler_params=pltpu.CompilerParams(vmem_limit_bytes=32 * 1024 * 1024),
        name="softmax",
    )(doc_lengths, soft_q, *pieces)

    lin_out = pl.pallas_call(
        functools.partial(across_kernel, bits - 1),
        out_shape=jax.ShapeDtypeStruct(lin_q.shape, BF16),
        in_specs=[SMEM] + [pl.BlockSpec(memory_space=pltpu.VMEM)] * 7,
        out_specs=pl.BlockSpec(memory_space=pltpu.VMEM),
        name="across",
    )(doc_lengths, lin_q, inside, log_decay, lin_gain.reshape(1, -1), first, prefix, far)
    return (lin_out, soft_out)


def solution(mesh):
    rows = P("ctx", "head")
    placed = (P(), rows, rows, rows, P("head", "ctx"), P("head"), rows, rows, rows)
    return jax.shard_map(
        local, mesh=mesh, in_specs=placed, out_specs=(rows, rows), check_vma=False
    )
```

time: 160 us -> 71.7 us (0.45)
  the two profiles are of different devices: /device:TPU:0 before, /device:TPU:30 now
where the time goes in v1:
time: 71.7 us; the launch traced here: 71.5 us
  Pallas kernels  47.7 us (67%)
  waiting for transfers between devices  17 us (24%)
  starting transfers between devices  4.3 us (6%)
  local copies, waits for them, and re-layouts  1.81 us (3%)
    pallas_call x1, Pallas kernels, local(): pl.pallas_call(functools.partial(softmax_kernel, count), out_shape=jax.Sh...  30.8 us
    ppermute x5, waiting for transfers between devices, swapped(): lax.ppermute(value, axis, [(i, i ^ 1 << bit) for i in range(lax.axis_size...  17 us
    pallas_call x1, Pallas kernels, local(): pl.pallas_call(inside_kernel, out_shape=jax.ShapeDtypeStruct(lin_q.shape,...  5.31 us
    pallas_call x1, Pallas kernels, local(): pl.pallas_call(functools.partial(across_kernel, bits - 1), out_shape=jax....  5.2 us
    pallas_call x1, Pallas kernels, local(): pl.pallas_call(states_kernel, out_shape=(msg, jax.ShapeDtypeStruct((max(b...  4.46 us
    ppermute x5, starting transfers between devices, swapped(): lax.ppermute(value, axis, [(i, i ^ 1 << bit) for i in range(lax.axis_size...  4.3 us
    pallas_call x1, Pallas kernels, local(): pl.pallas_call(body, out_shape=(msg, msg), in_specs=[pl.BlockSpec(memory_...  1.92 us
    unnamed x13, local copies, waits for them, and re-layouts  1.77 us
  transfers between devices with their start and end apart: 5, of which 3 were waited for; matrix products, arithmetic and copies ran while one was open for 0% of the time, Pallas kernels for 53%

profile of v1, /device:TPU:30, one launch (start us, length us, event | category | flops | bytes accessed | tf_op | source)
XLA Modules:
  0.0 71.5 jit_solution(10936501005463727475)
XLA Ops:
  0.6 0.0 copy-start.4
  0.6 4.5 %states.1 = (bf16[1040,128]{1,0:T(8,128)(2,1)}, bf16[1,1024,128]{2,1,0:T(8,128)(2,1)}) custom-call(s32[4]{0:T(128)} %lengths_ref.7, bf16[512,1024]{1,0:T(8,128)(2,1)} %keys_ref.3, bf16[512,1024]{1,0:T(8,128)(2,1)} %values_ref.3, f32[8,512]{1,0:T(8,128)} %decay_ref.5), custom_call_target="tpu_custom_call" | custom-call | tf_op jit(solution)/shard_map/states/pallas_call | solution.py:313
  5.1 0.0 copy-start.5
  5.1 0.5 collective-permute-start
  5.6 0.0 copy-done.4
  5.7 0.3 copy-done.5
  6.0 1.2 %collective-permute-start.2 = (bf16[512,256]{1,0:T(8,128)(2,1)S(1)}, bf16[512,256]{1,0:T(8,128)(2,1)S(1)}, u32[]{:S(2)}, u32[]{:S(2)}) collective-permute-start(bf16[512,256]{1,0:T(8,128)(2,1)S(1)} %constant_dynamic-update-slice_fusion.refs_0_), channel_id=1, source_target_pairs={{0,8},{8,0},{16,24},{24,16},{1,9},{9,1},{17,25},{25,17},{2,10},{10... | collective-permute-start | bytes 786440 | tf_op jit(solution)/shard_map/ppermute | solution.py:25
  7.3 7.3 %collective-permute-done.f = bf16[1040,128]{1,0:T(8,128)(2,1)S(1)} collective-permute-done((bf16[1040,128]{1,0:T(8,128)(2,1)}, bf16[1040,128]{1,0:T(8,128)(2,1)S(1)}, u32[]{:S(2)}, u32[]{:S(2)}) %collective-permute-start) | collective-permute-done | bytes 266272 | tf_op jit(solution)/shard_map/ppermute | solution.py:25
  14.6 0.0 copy-start.3
  14.6 0.7 copy-done.3
  15.3 1.9 %combine.1 = (bf16[1040,128]{1,0:T(8,128)(2,1)}, bf16[1040,128]{1,0:T(8,128)(2,1)}) custom-call(bf16[1040,128]{1,0:T(8,128)(2,1)} %get-tuple-element.7.t, bf16[1040,128]{1,0:T(8,128)(2,1)} %copy-done.3), custom_call_target="tpu_custom_call" | custom-call | tf_op jit(solution)/shard_map/combine/pallas_call | solution.py:339
  17.2 0.0 copy-start
  17.2 0.0 copy-start.1
  17.2 0.5 collective-permute-start.1
  17.7 1.5 %collective-permute-start.3 = (bf16[512,256]{1,0:T(8,128)(2,1)S(1)}, bf16[512,256]{1,0:T(8,128)(2,1)S(1)}, u32[]{:S(2)}, u32[]{:S(2)}) collective-permute-start(bf16[512,256]{1,0:T(8,128)(2,1)S(1)} %constant_dynamic-update-slice_fusion.refs_0_), channel_id=1, source_target_pairs={{0,16},{8,24},{16,0},{24,8},{1,17},{9,25},{17,1},{25,9},{2,18},{10... | collective-permute-start | bytes 786440 | tf_op jit(solution)/shard_map/ppermute | solution.py:25
  19.3 0.0 collective-permute-done.2.refs_1_
  19.3 0.5 collective-permute-start.4
  19.8 5.3 %inside.1.inside_ref = bf16[512,1024]{1,0:T(8,128)(2,1)} custom-call(s32[4]{0:T(128)} %lengths_ref.7, bf16[512,1024]{1,0:T(8,128)(2,1)} %queries_ref.4, bf16[512,1024]{1,0:T(8,128)(2,1)} %keys_ref.3, bf16[512,1024]{1,0:T(8,128)(2,1)} %values_ref.3, f32[8,512]{1,0:T(8,128)} %decay_ref.5), custom_call_target="tpu_custom_call" | custom-call | tf_op jit(solution)/shard_map/inside/pallas_call | solution.py:321
  25.1 6.9 %collective-permute-done.3.refs_2_ = bf16[512,256]{1,0:T(8,128)(2,1)S(1)} collective-permute-done((bf16[512,256]{1,0:T(8,128)(2,1)S(1)}, bf16[512,256]{1,0:T(8,128)(2,1)S(1)}, u32[]{:S(2)}, u32[]{:S(2)}) %collective-permute-start.3) | collective-permute-done | bytes 262176 | tf_op jit(solution)/shard_map/ppermute | solution.py:25
  32.0 2.8 %collective-permute-done.4.refs_3_ = bf16[512,256]{1,0:T(8,128)(2,1)S(1)} collective-permute-done((bf16[512,256]{1,0:T(8,128)(2,1)S(1)}, bf16[512,256]{1,0:T(8,128)(2,1)S(1)}, u32[]{:S(2)}, u32[]{:S(2)}) %collective-permute-start.4) | collective-permute-done | bytes 262176 | tf_op jit(solution)/shard_map/ppermute | solution.py:25
  34.8 0.0 copy-done
  34.8 0.0 copy-done.1
  34.8 30.8 %softmax.1 = bf16[512,1024]{1,0:T(8,128)(2,1)} custom-call(s32[4]{0:T(128)S(1)} %copy-done.1, bf16[512,1024]{1,0:T(8,128)(2,1)S(1)} %copy-done, bf16[512,256]{1,0:T(8,128)(2,1)S(1)} %constant_dynamic-update-slice_fusion.refs_0_, bf16[512,256]{1,0:T(8,128)(2,1)S(1)} %collective-permute-done.2.refs_1_, bf16[512,256]{1,0:T(8,128)(2,1)S(1)} %collective-permute-done.3.refs_2_, ...), custom_call_target="tpu_custom_call" | custom-call | tf_op jit(solution)/shard_map/softmax/pallas_call | solution.py:348
  65.6 0.0 collective-permute-done.1.far_ref
  65.6 0.0 copy-start.2
  65.6 0.7 copy-done.2
  66.3 5.2 %across.1 = bf16[512,1024]{1,0:T(8,128)(2,1)} custom-call(s32[4]{0:T(128)} %lengths_ref.7, bf16[512,1024]{1,0:T(8,128)(2,1)} %queries_ref.4, bf16[512,1024]{1,0:T(8,128)(2,1)} %inside.1.inside_ref, f32[8,512]{1,0:T(8,128)} %decay_ref.5, f32[1,1024]{1,0:T(1,128)} %bitcast.1, bf16[1,1024,128]{2,1,0:T(8,128)(2,1)} %get-tuple-element.6.first_ref, ...), custom_call_target="tpu_custom_call" | custom-call | tf_op jit(solution)/shard_map/across/pallas_call | solution.py:365
  (2 shorter events, 0.1 us)
Async XLA Ops:
  0.6 5.0 %copy-start.4 = (bf16[512,128]{1,0:T(8,128)(2,1)S(1)}, bf16[512,128]{1,0:T(8,128)(2,1)}, u32[]{:S(2)}) copy-start(bf16[512,128]{1,0:T(8,128)(2,1)} %param.16) | copy-start | bytes 393220
  5.1 0.9 %copy-start.5 = (bf16[512,128]{1,0:T(8,128)(2,1)S(1)}, bf16[512,128]{1,0:T(8,128)(2,1)}, u32[]{:S(2)}) copy-start(bf16[512,128]{1,0:T(8,128)(2,1)} %param.17) | copy-start | bytes 393220
  5.1 9.5 %collective-permute-start = (bf16[1040,128]{1,0:T(8,128)(2,1)}, bf16[1040,128]{1,0:T(8,128)(2,1)S(1)}, u32[]{:S(2)}, u32[]{:S(2)}) collective-permute-start(bf16[1040,128]{1,0:T(8,128)(2,1)} %get-tuple-element.7.t), channel_id=1, source_target_pairs={{0,8},{8,0},{16,24},{24,16},{1,9},{9,1},{17,25},{25,17},{2,10},{10... | collective-permute-start | bytes 798728 | tf_op jit(solution)/shard_map/ppermute | solution.py:25
  6.0 13.2 %collective-permute-start.2 = (bf16[512,256]{1,0:T(8,128)(2,1)S(1)}, bf16[512,256]{1,0:T(8,128)(2,1)S(1)}, u32[]{:S(2)}, u32[]{:S(2)}) collective-permute-start(bf16[512,256]{1,0:T(8,128)(2,1)S(1)} %constant_dynamic-update-slice_fusion.refs_0_), channel_id=1, source_target_pairs={{0,8},{8,0},{16,24},{24,16},{1,9},{9,1},{17,25},{25,17},{2,10},{10... | collective-permute-start | bytes 786440 | tf_op jit(solution)/shard_map/ppermute | solution.py:25
  14.6 0.7 copy-start.3
  17.2 17.6 %copy-start = (bf16[512,1024]{1,0:T(8,128)(2,1)S(1)}, bf16[512,1024]{1,0:T(8,128)(2,1)}, u32[]{:S(2)}) copy-start(bf16[512,1024]{1,0:T(8,128)(2,1)} %queries_ref.5) | copy-start | bytes 3145732
  17.2 17.6 %copy-start.1 = (s32[4]{0:T(128)S(1)}, s32[4]{0:T(128)}, u32[]{:S(2)}) copy-start(s32[4]{0:T(128)} %lengths_ref.7) | copy-start | bytes 52
  17.2 48.4 %collective-permute-start.1 = (bf16[1040,128]{1,0:T(8,128)(2,1)}, bf16[1040,128]{1,0:T(8,128)(2,1)S(1)}, u32[]{:S(2)}, u32[]{:S(2)}) collective-permute-start(bf16[1040,128]{1,0:T(8,128)(2,1)} %get-tuple-element.9), channel_id=1, source_target_pairs={{0,16},{8,24},{16,0},{24,8},{1,17},{9,25},{17,1},{25,9},{2,18},{10... | collective-permute-start | bytes 798728 | tf_op jit(solution)/shard_map/ppermute | solution.py:25
  17.7 14.2 %collective-permute-start.3 = (bf16[512,256]{1,0:T(8,128)(2,1)S(1)}, bf16[512,256]{1,0:T(8,128)(2,1)S(1)}, u32[]{:S(2)}, u32[]{:S(2)}) collective-permute-start(bf16[512,256]{1,0:T(8,128)(2,1)S(1)} %constant_dynamic-update-slice_fusion.refs_0_), channel_id=1, source_target_pairs={{0,16},{8,24},{16,0},{24,8},{1,17},{9,25},{17,1},{25,9},{2,18},{10... | collective-permute-start | bytes 786440 | tf_op jit(solution)/shard_map/ppermute | solution.py:25
  19.3 15.5 %collective-permute-start.4 = (bf16[512,256]{1,0:T(8,128)(2,1)S(1)}, bf16[512,256]{1,0:T(8,128)(2,1)S(1)}, u32[]{:S(2)}, u32[]{:S(2)}) collective-permute-start(bf16[512,256]{1,0:T(8,128)(2,1)S(1)} %collective-permute-done.2.refs_1_), channel_id=1, source_target_pairs={{0,16},{8,24},{16,0},{24,8},{1,17},{9,25},{17,1},{25,9},{2,18},{10... | collective-permute-start | bytes 786440 | tf_op jit(solution)/shard_map/ppermute | solution.py:25
  65.6 0.7 copy-start.2

commit v2 on v1

v2 whole, which is shorter than its diff:
```python
import functools

import jax
import jax.numpy as jnp
from jax import lax
from jax.experimental import pallas as pl
from jax.experimental.pallas import tpu as pltpu
from jax.sharding import PartitionSpec as P

KVH = 8
DH = 128
BLK = 256
KEYS = 512
ROWS = 256
PLACED = 4.0
LOW = -1e30
LOG2E = 1.4426950408889634
F32 = jnp.float32
BF16 = jnp.bfloat16
NT = (((1,), (1,)), ((), ()))
TN = (((0,), (0,)), ((), ()))
SMEM = pl.BlockSpec(memory_space=pltpu.SMEM)
ANY = pl.BlockSpec(memory_space=pl.ANY)
VMEM = pl.BlockSpec(memory_space=pltpu.VMEM)


def lasting(us):
    return pl.CostEstimate(flops=int(us * 1.1e9), bytes_accessed=0, transcendentals=0)


def swapped(value, axis, bit):
    return lax.ppermute(value, axis, [(i, i ^ 1 << bit) for i in range(lax.axis_size(axis))])


def bounds_of(lengths_ref):
    out, total = [], 0
    for d in range(lengths_ref.shape[0]):
        total = total + lengths_ref[d]
        out.append(total)
    return out


def doc_start(bounds, position):
    start = jnp.zeros_like(position)
    for bound in bounds:
        start = jnp.where(bound <= position, bound, start)
    return start


def log_sums(decay):
    rows = lax.broadcasted_iota(jnp.int32, (BLK, BLK), 0)
    cols = lax.broadcasted_iota(jnp.int32, (BLK, BLK), 1)
    upper = jnp.where(rows <= cols, 1.0, 0.0).astype(BF16)
    terms = []
    for _ in range(3):
        term = decay.astype(BF16).astype(F32)
        terms.append(term)
        decay = decay - term
    stacked = jnp.concatenate(terms, axis=0).astype(BF16)
    found = jnp.dot(stacked, upper, preferred_element_type=F32)
    count = decay.shape[0]
    return found[:count] + found[count : 2 * count] + found[2 * count :]


def states_kernel(lengths_ref, keys_ref, values_ref, decay_ref, msg_ref, first_ref, sums_ref):
    heads = decay_ref.shape[0]
    tokens = keys_ref.shape[0]
    base = lax.axis_index("ctx") * tokens
    bounds = bounds_of(lengths_ref)
    place = lax.broadcasted_iota(jnp.int32, (BLK, 1), 0)
    state = [None] * heads
    through = jnp.ones((heads, 1), F32)
    for b in range(tokens // BLK):
        s = base + b * BLK
        start_last = doc_start(bounds, s + BLK - 1)
        kept = jnp.where(start_last < s, 1.0, 0.0).astype(F32)
        sums = log_sums(decay_ref[:, b * BLK : (b + 1) * BLK])
        sums_ref[:, b * BLK : (b + 1) * BLK] = sums
        closing = sums[:, BLK - 1 : BLK]
        weights = jnp.transpose(jnp.exp(closing - sums), (1, 0))
        weights = jnp.where(s + place >= start_last, weights, 0.0)
        factor = kept * jnp.exp(closing)
        through = through * factor
        for h in range(heads):
            cols = slice(h * DH, (h + 1) * DH)
            keys = keys_ref[b * BLK : (b + 1) * BLK, cols].astype(F32)
            weighted = (keys * weights[:, h : h + 1]).astype(BF16)
            update = lax.dot_general(
                weighted, values_ref[b * BLK : (b + 1) * BLK, cols], TN, preferred_element_type=F32
            )
            if b == 0:
                state[h] = update
            else:
                state[h] = factor[h : h + 1, :] * state[h] + update
            if b < tokens // BLK - 1:
                first_ref[b, h * DH : (h + 1) * DH, :] = update.astype(BF16)
    for h in range(heads):
        msg_ref[h * DH : (h + 1) * DH, :] = state[h].astype(BF16)
    high = through.astype(BF16)
    low = (through - high.astype(F32)).astype(BF16)
    tail = jnp.concatenate([high.astype(F32), low.astype(F32)], axis=0)
    tail = jnp.broadcast_to(tail, (2 * heads, DH))
    extra = msg_ref.shape[0] - heads * DH
    if extra > 2 * heads:
        tail = jnp.concatenate([tail, jnp.zeros((extra - 2 * heads, DH), F32)], axis=0)
    msg_ref[heads * DH :, :] = tail.astype(BF16)


def inside_kernel(lengths_ref, queries_ref, keys_ref, values_ref, sums_ref, out_ref):
    heads = sums_ref.shape[0]
    tokens = keys_ref.shape[0]
    base = lax.axis_index("ctx") * tokens
    bounds = bounds_of(lengths_ref)
    rows = lax.broadcasted_iota(jnp.int32, (BLK, BLK), 0)
    cols = lax.broadcasted_iota(jnp.int32, (BLK, BLK), 1)
    place = lax.broadcasted_iota(jnp.int32, (BLK, 1), 0)
    for b in range(tokens // BLK):
        s = base + b * BLK
        start = doc_start(bounds, s + place) - s
        allowed = (cols <= rows) & (cols >= start)
        sums = sums_ref[:, b * BLK : (b + 1) * BLK]
        down = jnp.transpose(sums, (1, 0))
        here = slice(b * BLK, (b + 1) * BLK)
        for h in range(heads):
            there = slice(h * DH, (h + 1) * DH)
            spread = jnp.where(allowed, down[:, h : h + 1] - sums[h : h + 1, :], LOW)
            scores = lax.dot_general(
                queries_ref[here, there], keys_ref[here, there], NT, preferred_element_type=F32
            )
            scores = (scores * jnp.exp(spread)).astype(BF16)
            out_ref[here, there] = jnp.dot(
                scores, values_ref[here, there], preferred_element_type=F32
            ).astype(BF16)


def through_of(msg_ref, heads, h):
    high = msg_ref[heads * DH + h : heads * DH + h + 1, :].astype(F32)
    low = msg_ref[heads * DH + heads + h : heads * DH + heads + h + 1, :].astype(F32)
    return high + low


def joined(heads, early_ref, late_ref, swap, out_ref):
    def pick(here):
        one, two = early_ref[here, :].astype(F32), late_ref[here, :].astype(F32)
        return jnp.where(swap, two, one), jnp.where(swap, one, two)

    def through(h):
        high = pick(slice(heads * DH + h, heads * DH + h + 1))
        low = pick(slice(heads * DH + heads + h, heads * DH + heads + h + 1))
        return high[0] + low[0], high[1] + low[1]

    tails = []
    for h in range(heads):
        here = slice(h * DH, (h + 1) * DH)
        early, late = pick(here)
        early_through, late_through = through(h)
        out_ref[here, :] = (late_through * early + late).astype(BF16)
        tails.append(late_through * early_through)
    tail = jnp.concatenate(tails, axis=0)
    high = tail.astype(BF16).astype(F32)
    pieces = [high, tail - high]
    extra = out_ref.shape[0] - heads * DH - 2 * heads
    if extra:
        pieces.append(jnp.zeros((extra, DH), F32))
    out_ref[heads * DH :, :] = jnp.concatenate(pieces, axis=0).astype(BF16)


def upper_half(bit):
    return (lax.axis_index("ctx") // (1 << bit)) % 2 == 1


def total_kernel(heads, bit, total_ref, far_ref, new_total_ref):
    joined(heads, total_ref, far_ref, upper_half(bit), new_total_ref)


def prefix_kernel(heads, bit, prefix_ref, far_ref, new_prefix_ref):
    if bit == 1:
        first = jnp.where(upper_half(0), 1.0, 0.0).astype(F32)
        rows = prefix_ref.shape[0]
        tail = lax.broadcasted_iota(jnp.int32, (rows, DH), 0) - heads * DH
        own = prefix_ref[...].astype(F32) * first
        neutral = jnp.where((tail >= 0) & (tail < heads), 1.0 - first, 0.0)
        prefix_ref = (own + neutral).astype(BF16)

    @pl.when(upper_half(bit))
    def _():
        joined(heads, far_ref, prefix_ref, False, new_prefix_ref)

    @pl.when(jnp.logical_not(upper_half(bit)))
    def _():
        new_prefix_ref[...] = prefix_ref[...]


def across_kernel(bit, lengths_ref, queries_ref, inside_ref, sums_ref, gain_ref, first_ref, prefix_ref, far_ref, out_ref):
    heads = sums_ref.shape[0]
    tokens = queries_ref.shape[0]
    place_ctx = lax.axis_index("ctx")
    base = place_ctx * tokens
    upper = jnp.where(upper_half(bit), 1.0, 0.0).astype(F32)
    valid = jnp.where(upper_half(0), 1.0, 0.0).astype(F32) if bit == 1 else 1.0
    bounds = bounds_of(lengths_ref)
    place = lax.broadcasted_iota(jnp.int32, (BLK, 1), 0)
    state = []
    for h in range(heads):
        here = slice(h * DH, (h + 1) * DH)
        through = upper * (valid * through_of(prefix_ref, heads, h) + (1.0 - valid))
        state.append(valid * prefix_ref[here, :].astype(F32) + through * far_ref[here, :].astype(F32))
    for b in range(tokens // BLK):
        s = base + b * BLK
        here = slice(b * BLK, (b + 1) * BLK)
        start_last = doc_start(bounds, s + BLK - 1)
        kept = jnp.where(start_last < s, 1.0, 0.0).astype(F32)
        sums = sums_ref[:, here]
        factor = kept * jnp.exp(sums[:, BLK - 1 : BLK])
        entering = jnp.exp(jnp.transpose(sums, (1, 0)))
        entering = jnp.where(doc_start(bounds, s + place) < s, entering, 0.0)
        for h in range(heads):
            there = slice(h * DH, (h + 1) * DH)
            across = jnp.dot(queries_ref[here, there], state[h].astype(BF16), preferred_element_type=F32)
            raw = inside_ref[here, there].astype(F32) + across * entering[:, h : h + 1]
            scale = lax.rsqrt(jnp.mean(raw * raw, axis=1, keepdims=True) + 1e-06)
            out_ref[here, there] = (raw * scale * gain_ref[:, there]).astype(BF16)
            if b < tokens // BLK - 1:
                state[h] = factor[h : h + 1, :] * state[h] + first_ref[b, there, :].astype(F32)


def softmax_kernel(count, lengths_ref, queries_ref, *refs):
    pieces = refs[:count]
    out_ref, keys, values, scores, tops, totals, sems = refs[count:]
    tokens = queries_ref.shape[0]
    heads = queries_ref.shape[1] // DH
    place_ctx = lax.axis_index("ctx")
    base = place_ctx * tokens
    copies = []
    for m in range(count):
        origin = jnp.int32(0)
        bit = 1
        while bit < count:
            mine = (place_ctx // bit) % 2
            origin = origin + bit * (1 - mine if m & bit else mine)
            bit *= 2
        at = pl.ds(pl.multiple_of(KEYS + origin * tokens, 128), tokens)
        copies.append(pltpu.make_async_copy(pieces[m].at[:, :DH], keys.at[at, :], sems.at[0, m]))
        copies.append(pltpu.make_async_copy(pieces[m].at[:, DH:], values.at[at, :DH], sems.at[1, m]))
    for copy in copies:
        copy.start()
    keys[:KEYS, :] = jnp.zeros((KEYS, DH), BF16)
    values[:KEYS, :DH] = jnp.zeros((KEYS, DH), BF16)
    values[:, DH:] = jnp.ones((values.shape[0], DH), BF16)
    for copy in copies:
        copy.wait()
    bounds = bounds_of(lengths_ref)
    place = lax.broadcasted_iota(jnp.int32, (ROWS, 1), 0)
    spots = lax.broadcasted_iota(jnp.int32, (ROWS, KEYS), 1)
    factor = LOG2E * DH**-0.5
    parts = KEYS // 128

    def row_block(block, _):
        r0 = pl.multiple_of(block * ROWS, ROWS)
        s = base + r0
        row_start = doc_start(bounds, s + place)
        start_half = doc_start(bounds, s + ROWS // 2)
        start_last = doc_start(bounds, s + ROWS - 1)
        steps = (s + ROWS - doc_start(bounds, s) + KEYS - 1) // KEYS

        def first_of(i):
            return s + ROWS - KEYS * (i + 1)

        def at(i):
            return pl.ds(pl.multiple_of(KEYS + first_of(i), 128), KEYS)

        def bias_of(i):
            spot = first_of(i) + spots
            return jnp.where((spot >= row_start) & (spot <= s + place), 0.0, LOW)

        def query(h, rows=ROWS):
            return queries_ref[pl.ds(r0, rows), h * DH : (h + 1) * DH]

        def weighted(found, top):
            spread = [found[:, p * 128 : (p + 1) * 128] * factor - top for p in range(parts)]
            return jnp.concatenate([jnp.exp2(x.astype(BF16)) for x in spread], axis=1)

        bias = bias_of(0)
        key, value = keys[at(0), :], values[at(0), :]
        for h in range(heads):
            here = slice(h * ROWS, (h + 1) * ROWS)
            found = lax.dot_general(query(h), key, NT, preferred_element_type=F32) + bias
            scores[here, :] = found
            top = found[:, :128]
            for p in range(1, parts):
                top = jnp.maximum(top, found[:, p * 128 : (p + 1) * 128])
            top = jnp.max(top, axis=1, keepdims=True) * factor - PLACED
            tops[here, :] = jnp.broadcast_to(top, (ROWS, 128))
        for h in range(heads):
            here = slice(h * ROWS, (h + 1) * ROWS)
            totals[here, :] = jnp.dot(
                weighted(scores[here, :], tops[here, :]), value, preferred_element_type=F32
            )

        def further(i, _):
            def add(bias, rows):
                key, value = keys[at(i), :], values[at(i), :]
                for h in range(heads):
                    here = slice(h * ROWS, h * ROWS + rows)
                    found = lax.dot_general(query(h, rows), key, NT, preferred_element_type=F32)
                    if bias is not None:
                        found = found + bias[:rows]
                    totals[here, :] += jnp.dot(
                        weighted(found, tops[here, :]), value, preferred_element_type=F32
                    )

            whole = first_of(i) >= start_last
            half = first_of(i) + KEYS <= start_half

            @pl.when(whole)
            def _():
                add(None, ROWS)

            @pl.when(jnp.logical_not(whole) & jnp.logical_not(half))
            def _():
                add(bias_of(i), ROWS)

            @pl.when(half)
            def _():
                add(bias_of(i), ROWS // 2)

            return 0

        lax.fori_loop(1, steps, further, 0)

        def settled(rows):
            return jnp.max(totals[rows, DH:]) < 2.0**115

        @pl.when(jnp.logical_not(settled(slice(0, heads * ROWS))))
        def _():
            def one(h, _):
                here = pl.ds(pl.multiple_of(h * ROWS, ROWS), ROWS)

                @pl.when(jnp.logical_not(settled(here)))
                def _():
                    lone = queries_ref[pl.ds(r0, ROWS), pl.ds(pl.multiple_of(h * DH, DH), DH)]

                    def found_of(i):
                        found = lax.dot_general(lone, keys[at(i), :], NT, preferred_element_type=F32)
                        return found + bias_of(i)

                    def highest(i, top):
                        return jnp.maximum(top, jnp.max(found_of(i), axis=1, keepdims=True))

                    top = lax.fori_loop(0, steps, highest, jnp.full((ROWS, 1), LOW, F32))
                    totals[here, :] = jnp.zeros((ROWS, 2 * DH), F32)

                    def add(i, _):
                        weights = jnp.exp2((found_of(i) - top) * factor).astype(BF16)
                        totals[here, :] += jnp.dot(weights, values[at(i), :], preferred_element_type=F32)
                        return 0

                    lax.fori_loop(0, steps, add, 0)

                return 0

            lax.fori_loop(0, heads, one, 0)

        for h in range(heads):
            here = slice(h * ROWS, (h + 1) * ROWS)
            out_ref[pl.ds(r0, ROWS), h * DH : (h + 1) * DH] = (
                totals[here, :DH] / totals[here, DH:]
            ).astype(BF16)
        return 0

    lax.fori_loop(0, tokens // ROWS, row_block, 0)


def local(doc_lengths, lin_q, lin_k, lin_v, log_decay, lin_gain, soft_q, soft_k, soft_v):
    tokens = lin_q.shape[0]
    heads = lin_gain.shape[0] // DH
    count = lax.axis_size("ctx")
    bits = count.bit_length() - 1
    blocks = tokens // BLK

    head_place = lax.axis_index("head")
    own_keys, own_values = soft_k, soft_v
    for bit in range((lax.axis_size("head") // KVH).bit_length() - 1):
        far_keys, far_values = swapped((own_keys, own_values), "head", bit)
        upper = head_place // (1 << bit) % 2 == 1

        def beside(own, far):
            return jnp.where(upper, jnp.concatenate([far, own], axis=1), jnp.concatenate([own, far], axis=1))

        own_keys, own_values = beside(own_keys, far_keys), beside(own_values, far_values)
    pieces = [jnp.concatenate([own_keys, own_values], axis=1)]
    for bit in range(bits):
        pieces = pieces + [swapped(piece, "ctx", bit) for piece in pieces]

    msg_rows = heads * DH + -(-2 * heads // 16) * 16
    msg = jax.ShapeDtypeStruct((msg_rows, DH), BF16)
    total, first, sums = pl.pallas_call(
        states_kernel,
        out_shape=(
            msg,
            jax.ShapeDtypeStruct((max(blocks - 1, 1), heads * DH, DH), BF16),
            jax.ShapeDtypeStruct(log_decay.shape, F32),
        ),
        in_specs=[SMEM] + [VMEM] * 3,
        out_specs=(VMEM,) * 3,
        cost_estimate=lasting(2.5),
        name="states",
    )(doc_lengths, lin_k, lin_v, log_decay)

    inside = pl.pallas_call(
        inside_kernel,
        out_shape=jax.ShapeDtypeStruct(lin_q.shape, BF16),
        in_specs=[SMEM] + [VMEM] * 4,
        out_specs=VMEM,
        cost_estimate=lasting(4),
        name="inside",
    )(doc_lengths, lin_q, lin_k, lin_v, sums)

    prefix = None
    for bit in range(bits - 1):
        far = swapped(total, "ctx", bit)
        if bit == 0:
            prefix = far
        else:
            prefix = pl.pallas_call(
                functools.partial(prefix_kernel, heads, bit),
                out_shape=msg,
                in_specs=[VMEM] * 2,
                out_specs=VMEM,
                name="prefix",
            )(prefix, far)
        total = pl.pallas_call(
            functools.partial(total_kernel, heads, bit),
            out_shape=msg,
            in_specs=[VMEM] * 2,
            out_specs=VMEM,
            cost_estimate=lasting(1),
            name="total",
        )(total, far)
    far = swapped(total, "ctx", bits - 1)

    soft_out = pl.pallas_call(
        functools.partial(softmax_kernel, count),
        out_shape=jax.ShapeDtypeStruct(soft_q.shape, BF16),
        in_specs=[SMEM, VMEM] + [ANY] * count,
        out_specs=VMEM,
        scratch_shapes=[
            pltpu.VMEM((KEYS + count * tokens, DH), BF16),
            pltpu.VMEM((KEYS + count * tokens, 2 * DH), BF16),
            pltpu.VMEM((heads * ROWS, KEYS), F32),
            pltpu.VMEM((heads * ROWS, 128), F32),
            pltpu.VMEM((heads * ROWS, 2 * DH), F32),
            pltpu.SemaphoreType.DMA((2, count)),
        ],
        compiler_params=pltpu.CompilerParams(vmem_limit_bytes=32 * 1024 * 1024),
        cost_estimate=lasting(12),
        name="softmax",
    )(doc_lengths, soft_q, *pieces)

    lin_out = pl.pallas_call(
        functools.partial(across_kernel, bits - 1),
        out_shape=jax.ShapeDtypeStruct(lin_q.shape, BF16),
        in_specs=[SMEM] + [VMEM] * 7,
        out_specs=VMEM,
        cost_estimate=lasting(3),
        name="across",
    )(doc_lengths, lin_q, inside, sums, lin_gain.reshape(1, -1), first, prefix, far)
    return (lin_out, soft_out)


def solution(mesh):
    rows = P("ctx", "head")
    placed = (P(), rows, rows, rows, P("head", "ctx"), P("head"), rows, rows, rows)
    return jax.shard_map(
        local, mesh=mesh, in_specs=placed, out_specs=(rows, rows), check_vma=False
    )
```

time: 71.7 us -> 37.6 us (0.52)
  the two profiles are of different devices: /device:TPU:30 before, /device:TPU:28 now
where the time goes in v2:
time: 37.6 us; the launch traced here: 37.3 us
  Pallas kernels  27.4 us (73%)
  starting transfers between devices  4.62 us (12%)
  local copies, waits for them, and re-layouts  2.41 us (6%)
  waiting for transfers between devices  2.17 us (6%)
  between operations  0.7 us (2%)
    pallas_call x1, Pallas kernels, local(): pl.pallas_call(functools.partial(softmax_kernel, count), out_shape=jax.Sh...  11.6 us
    pallas_call x1, Pallas kernels, local(): pl.pallas_call(functools.partial(across_kernel, bits - 1), out_shape=jax....  5.03 us
    ppermute x5, starting transfers between devices, swapped(): lax.ppermute(value, axis, [(i, i ^ 1 << bit) for i in range(lax.axis_size...  4.62 us
    pallas_call x1, Pallas kernels, local(): pl.pallas_call(inside_kernel, out_shape=jax.ShapeDtypeStruct(lin_q.shape,...  4.57 us
    pallas_call x1, Pallas kernels, local(): pl.pallas_call(states_kernel, out_shape=(msg, jax.ShapeDtypeStruct((max(b...  4.31 us
    unnamed x11, local copies, waits for them, and re-layouts  2.38 us
    ppermute x5, waiting for transfers between devices, swapped(): lax.ppermute(value, axis, [(i, i ^ 1 << bit) for i in range(lax.axis_size...  2.17 us
    pallas_call x1, Pallas kernels, local(): pl.pallas_call(functools.partial(total_kernel, heads, bit), out_shape=msg...  1.89 us
  transfers between devices with their start and end apart: 5, of which 2 were waited for; matrix products, arithmetic and copies ran while one was open for 0% of the time, Pallas kernels for 60%

profile of v2, /device:TPU:28, one launch (start us, length us, event | category | flops | bytes accessed | tf_op | source)
XLA Modules:
  0.0 37.3 jit_solution(2632584734006093315)
XLA Ops:
  0.6 0.0 copy-start.2
  0.6 1.0 %constant_dynamic-update-slice_fusion.1 = bf16[512,256]{1,0:T(8,128)(2,1)S(1)} fusion(bf16[512,128]{1,0:T(8,128)(2,1)} %param.16), kind=kLoop, calls=%fused_computation.1 | loop fusion | bytes 262144
  1.6 0.0 copy-done.2
  1.7 1.6 %collective-permute-start.2 = (bf16[512,256]{1,0:T(8,128)(2,1)S(1)}, bf16[512,256]{1,0:T(8,128)(2,1)S(1)}, u32[]{:S(2)}, u32[]{:S(2)}) collective-permute-start(bf16[512,256]{1,0:T(8,128)(2,1)S(1)} %constant_dynamic-update-slice_fusion.refs_0_), channel_id=1, source_target_pairs={{0,8},{8,0},{16,24},{24,16},{1,9},{9,1},{17,25},{25,17},{2,10},{10... | collective-permute-start | bytes 786440 | tf_op jit(solution)/shard_map/ppermute | solution.py:32
  3.2 0.5 %collective-permute-start.3 = (bf16[512,256]{1,0:T(8,128)(2,1)S(1)}, bf16[512,256]{1,0:T(8,128)(2,1)S(1)}, u32[]{:S(2)}, u32[]{:S(2)}) collective-permute-start(bf16[512,256]{1,0:T(8,128)(2,1)S(1)} %constant_dynamic-update-slice_fusion.refs_0_), channel_id=1, source_target_pairs={{0,16},{8,24},{16,0},{24,8},{1,17},{9,25},{17,1},{25,9},{2,18},{10... | collective-permute-start | bytes 786440 | tf_op jit(solution)/shard_map/ppermute | solution.py:32
  3.7 4.3 %states.1 = (bf16[1040,128]{1,0:T(8,128)(2,1)}, bf16[1,1024,128]{2,1,0:T(8,128)(2,1)}, f32[8,512]{1,0:T(8,128)}) custom-call(s32[4]{0:T(128)} %lengths_ref.7, bf16[512,1024]{1,0:T(8,128)(2,1)} %keys_ref.3, bf16[512,1024]{1,0:T(8,128)(2,1)} %values_ref.3, f32[8,512]{1,0:T(8,128)} %decay_ref.1), custom_call_target="tpu_custom_call" | custom-call | flops 2750000128 | tf_op jit(solution)/shard_map/states/pallas_call | solution.py:397
  8.0 0.5 %collective-permute-start = (bf16[1040,128]{1,0:T(8,128)(2,1)}, bf16[1040,128]{1,0:T(8,128)(2,1)S(1)}, u32[]{:S(2)}, u32[]{:S(2)}) collective-permute-start(bf16[1040,128]{1,0:T(8,128)(2,1)} %get-tuple-element.7.total_ref), channel_id=1, source_target_pairs={{0,8},{8,0},{16,24},{24,16},{1,9},{9,1},{17,25},{25,17},{2,10},{10... | collective-permute-start | bytes 798728 | tf_op jit(solution)/shard_map/ppermute | solution.py:32
  8.6 1.2 %collective-permute-done.2.refs_1_ = bf16[512,256]{1,0:T(8,128)(2,1)S(1)} collective-permute-done((bf16[512,256]{1,0:T(8,128)(2,1)S(1)}, bf16[512,256]{1,0:T(8,128)(2,1)S(1)}, u32[]{:S(2)}, u32[]{:S(2)}) %collective-permute-start.2) | collective-permute-done | bytes 262176 | tf_op jit(solution)/shard_map/ppermute | solution.py:32
  9.8 0.5 %collective-permute-start.4 = (bf16[512,256]{1,0:T(8,128)(2,1)S(1)}, bf16[512,256]{1,0:T(8,128)(2,1)S(1)}, u32[]{:S(2)}, u32[]{:S(2)}) collective-permute-start(bf16[512,256]{1,0:T(8,128)(2,1)S(1)} %collective-permute-done.2.refs_1_), channel_id=1, source_target_pairs={{0,16},{8,24},{16,0},{24,8},{1,17},{9,25},{17,1},{25,9},{2,18},{10... | collective-permute-start | bytes 786440 | tf_op jit(solution)/shard_map/ppermute | solution.py:32
  10.3 4.6 %inside.1.inside_ref = bf16[512,1024]{1,0:T(8,128)(2,1)} custom-call(s32[4]{0:T(128)} %lengths_ref.7, bf16[512,1024]{1,0:T(8,128)(2,1)} %queries_ref.4, bf16[512,1024]{1,0:T(8,128)(2,1)} %keys_ref.3, bf16[512,1024]{1,0:T(8,128)(2,1)} %values_ref.3, f32[8,512]{1,0:T(8,128)} %get-tuple-element.5.sums_ref), custom_call_target="tpu_custom_call" | custom-call | flops 4400000000 | tf_op jit(solution)/shard_map/inside/pallas_call | solution.py:410
  14.8 0.0 copy-start
  14.9 0.0 copy-start.1
  14.9 1.0 %collective-permute-done.far_ref.prefix_ref = bf16[1040,128]{1,0:T(8,128)(2,1)S(1)} collective-permute-done((bf16[1040,128]{1,0:T(8,128)(2,1)}, bf16[1040,128]{1,0:T(8,128)(2,1)S(1)}, u32[]{:S(2)}, u32[]{:S(2)}) %collective-permute-start) | collective-permute-done | bytes 266272 | tf_op jit(solution)/shard_map/ppermute | solution.py:32
  15.8 0.0 copy-start.3
  15.8 0.7 %copy-done.3 = bf16[1040,128]{1,0:T(8,128)(2,1)} copy-done((bf16[1040,128]{1,0:T(8,128)(2,1)}, bf16[1040,128]{1,0:T(8,128)(2,1)S(1)}, u32[]{:S(2)}) %copy-start.3) | copy-done | bytes 266264
  16.5 1.9 %total.1 = bf16[1040,128]{1,0:T(8,128)(2,1)} custom-call(bf16[1040,128]{1,0:T(8,128)(2,1)} %get-tuple-element.7.total_ref, bf16[1040,128]{1,0:T(8,128)(2,1)} %copy-done.3), custom_call_target="tpu_custom_call" | custom-call | flops 1100000000 | tf_op jit(solution)/shard_map/total/pallas_call | solution.py:432
  18.4 1.5 %collective-permute-start.1 = (bf16[1040,128]{1,0:T(8,128)(2,1)}, bf16[1040,128]{1,0:T(8,128)(2,1)S(1)}, u32[]{:S(2)}, u32[]{:S(2)}) collective-permute-start(bf16[1040,128]{1,0:T(8,128)(2,1)} %total.1), channel_id=1, source_target_pairs={{0,16},{8,24},{16,0},{24,8},{1,17},{9,25},{17,1},{25,9},{2,18},{10... | collective-permute-start | bytes 798728 | tf_op jit(solution)/shard_map/ppermute | solution.py:32
  19.9 0.0 collective-permute-done.3.refs_2_
  19.9 0.0 collective-permute-done.4.refs_3_
  19.9 0.0 copy-done
  19.9 0.0 copy-done.1
  19.9 11.6 %softmax.1 = bf16[512,1024]{1,0:T(8,128)(2,1)} custom-call(s32[4]{0:T(128)S(1)} %copy-done.1, bf16[512,1024]{1,0:T(8,128)(2,1)S(1)} %copy-done, bf16[512,256]{1,0:T(8,128)(2,1)S(1)} %constant_dynamic-update-slice_fusion.refs_0_, bf16[512,256]{1,0:T(8,128)(2,1)S(1)} %collective-permute-done.2.refs_1_, bf16[512,256]{1,0:T(8,128)(2,1)S(1)} %collective-permute-done.3.refs_2_, ...), custom_call_target="tpu_custom_call" | custom-call | flops 13200000000 | tf_op jit(solution)/shard_map/softmax/pallas_call | solution.py:442
  31.6 0.0 collective-permute-done.1.far_ref
  31.6 0.0 copy-start.4
  31.6 0.7 %copy-done.4 = bf16[1040,128]{1,0:T(8,128)(2,1)} copy-done((bf16[1040,128]{1,0:T(8,128)(2,1)}, bf16[1040,128]{1,0:T(8,128)(2,1)S(1)}, u32[]{:S(2)}) %copy-start.4) | copy-done | bytes 266264
  32.3 5.0 %across.1 = bf16[512,1024]{1,0:T(8,128)(2,1)} custom-call(s32[4]{0:T(128)} %lengths_ref.7, bf16[512,1024]{1,0:T(8,128)(2,1)} %queries_ref.4, bf16[512,1024]{1,0:T(8,128)(2,1)} %inside.1.inside_ref, f32[8,512]{1,0:T(8,128)} %get-tuple-element.5.sums_ref, f32[1,1024]{1,0:T(1,128)} %bitcast.1, bf16[1,1024,128]{2,1,0:T(8,128)(2,1)} %get-tuple-element.6.first_ref, ...), custom_call_target="tpu_custom_call" | custom-call | flops 3300000000 | tf_op jit(solution)/shard_map/across/pallas_call | solution.py:460
  (1 shorter events, 0.0 us)
Async XLA Ops:
  0.6 1.0 %copy-start.2 = (bf16[512,128]{1,0:T(8,128)(2,1)S(1)}, bf16[512,128]{1,0:T(8,128)(2,1)}, u32[]{:S(2)}) copy-start(bf16[512,128]{1,0:T(8,128)(2,1)} %param.17) | copy-start | bytes 393220
  1.7 8.1 %collective-permute-start.2 = (bf16[512,256]{1,0:T(8,128)(2,1)S(1)}, bf16[512,256]{1,0:T(8,128)(2,1)S(1)}, u32[]{:S(2)}, u32[]{:S(2)}) collective-permute-start(bf16[512,256]{1,0:T(8,128)(2,1)S(1)} %constant_dynamic-update-slice_fusion.refs_0_), channel_id=1, source_target_pairs={{0,8},{8,0},{16,24},{24,16},{1,9},{9,1},{17,25},{25,17},{2,10},{10... | collective-permute-start | bytes 786440 | tf_op jit(solution)/shard_map/ppermute | solution.py:32
  3.2 16.7 %collective-permute-start.3 = (bf16[512,256]{1,0:T(8,128)(2,1)S(1)}, bf16[512,256]{1,0:T(8,128)(2,1)S(1)}, u32[]{:S(2)}, u32[]{:S(2)}) collective-permute-start(bf16[512,256]{1,0:T(8,128)(2,1)S(1)} %constant_dynamic-update-slice_fusion.refs_0_), channel_id=1, source_target_pairs={{0,16},{8,24},{16,0},{24,8},{1,17},{9,25},{17,1},{25,9},{2,18},{10... | collective-permute-start | bytes 786440 | tf_op jit(solution)/shard_map/ppermute | solution.py:32
  8.0 7.8 %collective-permute-start = (bf16[1040,128]{1,0:T(8,128)(2,1)}, bf16[1040,128]{1,0:T(8,128)(2,1)S(1)}, u32[]{:S(2)}, u32[]{:S(2)}) collective-permute-start(bf16[1040,128]{1,0:T(8,128)(2,1)} %get-tuple-element.7.total_ref), channel_id=1, source_target_pairs={{0,8},{8,0},{16,24},{24,16},{1,9},{9,1},{17,25},{25,17},{2,10},{10... | collective-permute-start | bytes 798728 | tf_op jit(solution)/shard_map/ppermute | solution.py:32
  9.8 10.2 %collective-permute-start.4 = (bf16[512,256]{1,0:T(8,128)(2,1)S(1)}, bf16[512,256]{1,0:T(8,128)(2,1)S(1)}, u32[]{:S(2)}, u32[]{:S(2)}) collective-permute-start(bf16[512,256]{1,0:T(8,128)(2,1)S(1)} %collective-permute-done.2.refs_1_), channel_id=1, source_target_pairs={{0,16},{8,24},{16,0},{24,8},{1,17},{9,25},{17,1},{25,9},{2,18},{10... | collective-permute-start | bytes 786440 | tf_op jit(solution)/shard_map/ppermute | solution.py:32
  14.8 5.1 %copy-start = (bf16[512,1024]{1,0:T(8,128)(2,1)S(1)}, bf16[512,1024]{1,0:T(8,128)(2,1)}, u32[]{:S(2)}) copy-start(bf16[512,1024]{1,0:T(8,128)(2,1)} %queries_ref.5) | copy-start | bytes 3145732
  14.9 5.1 %copy-start.1 = (s32[4]{0:T(128)S(1)}, s32[4]{0:T(128)}, u32[]{:S(2)}) copy-start(s32[4]{0:T(128)} %lengths_ref.7) | copy-start | bytes 52
  15.8 0.7 %copy-start.3 = (bf16[1040,128]{1,0:T(8,128)(2,1)}, bf16[1040,128]{1,0:T(8,128)(2,1)S(1)}, u32[]{:S(2)}) copy-start(bf16[1040,128]{1,0:T(8,128)(2,1)S(1)} %collective-permute-done.far_ref.prefix_ref) | copy-start | bytes 798724
  18.4 13.2 %collective-permute-start.1 = (bf16[1040,128]{1,0:T(8,128)(2,1)}, bf16[1040,128]{1,0:T(8,128)(2,1)S(1)}, u32[]{:S(2)}, u32[]{:S(2)}) collective-permute-start(bf16[1040,128]{1,0:T(8,128)(2,1)} %total.1), channel_id=1, source_target_pairs={{0,16},{8,24},{16,0},{24,8},{1,17},{9,25},{17,1},{25,9},{2,18},{10... | collective-permute-start | bytes 798728 | tf_op jit(solution)/shard_map/ppermute | solution.py:32
  31.6 0.7 %copy-start.4 = (bf16[1040,128]{1,0:T(8,128)(2,1)}, bf16[1040,128]{1,0:T(8,128)(2,1)S(1)}, u32[]{:S(2)}) copy-start(bf16[1040,128]{1,0:T(8,128)(2,1)S(1)} %collective-permute-done.1.far_ref) | copy-start | bytes 798724
